TPU v7x, 32 devices: a whole 2x2x4 slice. The times are simulated.
32 devices in a mesh: beam: 2 (over x), wide: 16 (over z, y, core).
Axes of the slice: x: 2, y: 2, z: 4, core: 2. Of those that a mesh axis runs over, the one named last changes fastest.
Arguments:
- filterbank: bfloat16 [2, 4096, 4096], P('beam', 'wide'), parts along dimension 0, may hold values from -100 to 100
- channel_mask: int32 [8192], P(('beam', 'wide')), parts along dimension 0, may hold values 0 or 1
- band_edges: int32 [7], replicated, may hold values from 385 to 3711, as said below
- dm_delays: int32 [16], replicated, may hold values from 0 to 2047
Outputs:
- series: float32 [2, 16, 4096], P('beam', 'wide'), parts along dimension 0
There are 2 independent parts, one for each index of `beam`. A program takes and returns all parts, laid end to end along the dimension named above; an argument that names none is the same for every part. Nothing has to cross between parts.
Inputs may be any that keep to these rules, and one draw needn't show every extreme that they name: `band_edges`: strictly increasing; entry i lies at (i + 1) * 512 up to a shift of less than 128.
All inputs are finite; a program needn't handle non-finite values. No bound on the sum of `channel_mask` on one device may be relied on, other than what follows from the above.
Results may differ from a plain program's by a relative error of at most 0.0063.
Values may be sent and summed in bfloat16 or wider, within the bound.
No kernel may reach another device: no remote copies, remote signals or barrier semaphores. Data moves between devices by JAX's collectives and lax.ppermute only.
A program may use at most 64 MiB of HBM per device.

v0:
```python
import math

import jax
import jax.numpy as jnp
from jax import lax
from jax.sharding import PartitionSpec as P

C = 4096
NBLK = 8


def delay_fractions(channel_count, total_channels):
    channel_ids = jnp.arange(channel_count, dtype=jnp.int32)
    ratio = 0.5 + 0.5 * (channel_ids.astype(jnp.float32) + 0.5) / total_channels
    return (1.0 / (ratio * ratio) - 1.0) / 3.0


def noise_floors(band_power, band_edges, channels):
    bounds = jnp.concatenate(
        [jnp.zeros((1,), jnp.int32), band_edges, jnp.full((1,), channels, jnp.int32)]
    )
    widths = (bounds[1:] - bounds[:-1]).astype(jnp.float32)
    return jnp.sqrt(band_power / widths[None, :, None] + 1e-05)


def forward_tables(first_bin, bin_count, samples):
    bin_ids = first_bin + jnp.arange(bin_count, dtype=jnp.int32)
    times = jnp.arange(samples, dtype=jnp.int32)
    product = bin_ids[:, None] * times[None, :] % samples
    angle = product.astype(jnp.float32) * (2.0 * math.pi / samples)
    tables = jnp.stack([jnp.cos(angle), -jnp.sin(angle)], axis=0)
    return tables.reshape(2 * bin_count, samples).astype(jnp.bfloat16)


def inverse_tables(first_bin, bin_count, samples, channels):
    bin_ids = first_bin + jnp.arange(bin_count, dtype=jnp.int32)
    times = jnp.arange(samples, dtype=jnp.int32)
    product = bin_ids[:, None] * times[None, :] % samples
    angle = product.astype(jnp.float32) * (2.0 * math.pi / samples)
    weight = jnp.where(bin_ids == 0, 1.0, 2.0).astype(jnp.float32) / (samples * math.sqrt(channels))
    tables = jnp.stack(
        [weight[:, None] * jnp.cos(angle), -weight[:, None] * jnp.sin(angle)], axis=1
    )
    return tables.reshape(2 * bin_count, samples).astype(jnp.bfloat16)


def phase_tables(first_bin, bin_count, fractions, dm_delays, samples):
    bin_ids = first_bin + jnp.arange(bin_count, dtype=jnp.int32)
    cycles = (bin_ids[:, None] * dm_delays[None, :]).astype(jnp.float32)
    angle = cycles[:, None, :] * fractions[None, :, None] * (2.0 * math.pi / samples)
    return (jnp.cos(angle).astype(jnp.bfloat16), jnp.sin(angle).astype(jnp.bfloat16))


def spectrum_block(rows_flat, first_bin, bin_count, samples):
    tables = forward_tables(first_bin, bin_count, samples)
    block = lax.dot_general(
        tables, rows_flat, (((1,), (1,)), ((), ())), preferred_element_type=jnp.float32
    )
    return block.astype(jnp.bfloat16)


def dedisperse_block(spec_real, spec_imag, cos_tab, sin_tab):
    real_part = jnp.einsum(
        "fbc,fcd->fbd", spec_real, cos_tab, preferred_element_type=jnp.float32
    ) - jnp.einsum("fbc,fcd->fbd", spec_imag, sin_tab, preferred_element_type=jnp.float32)
    imag_part = jnp.einsum(
        "fbc,fcd->fbd", spec_real, sin_tab, preferred_element_type=jnp.float32
    ) + jnp.einsum("fbc,fcd->fbd", spec_imag, cos_tab, preferred_element_type=jnp.float32)
    return jnp.stack([real_part, imag_part], axis=1)


def body(filterbank, channel_mask, band_edges, dm_delays):
    beams, local_channels, samples = filterbank.shape
    group_size = lax.axis_size("wide")
    position = lax.axis_index("wide")
    first_channel = position * local_channels
    bands = band_edges.shape[0] + 1
    signal = filterbank.astype(jnp.float32).reshape(beams, local_channels, NBLK, samples // NBLK)
    power = jnp.mean(signal * signal, axis=3)
    channel_ids = first_channel + jnp.arange(local_channels, dtype=jnp.int32)
    band_ids = jnp.sum((band_edges[None, :] <= channel_ids[:, None]).astype(jnp.int32), axis=1)
    member = (band_ids[:, None] == jnp.arange(bands, dtype=jnp.int32)[None, :]).astype(jnp.float32)
    keep = channel_mask.astype(jnp.float32)
    local_power = jnp.einsum(
        "cj,bck->bjk", member * keep[:, None], power, precision=lax.Precision.HIGHEST
    )
    band_power = lax.psum(local_power, "wide")
    floors = noise_floors(band_power, band_edges, C)
    channel_floor = jnp.einsum("cj,bjk->bck", member, floors, precision=lax.Precision.HIGHEST)
    cleaned = (
        (signal / channel_floor[..., None] * keep[None, :, None, None])
        .reshape(beams, local_channels, samples)
        .astype(jnp.bfloat16)
    )
    rows_flat = cleaned.reshape(beams * local_channels, samples)
    bins = samples // 4
    local_bins = bins // group_size
    total_dms = dm_delays.shape[0]
    local_dms = total_dms // group_size
    dft_step = math.gcd(bins, 512)

    def fill_spectrum(step, buffer):
        first_bin = step * dft_step
        block = spectrum_block(rows_flat, first_bin, dft_step, samples).reshape(
            2, dft_step, beams, local_channels
        )
        return lax.dynamic_update_slice_in_dim(buffer, block, first_bin, 1)

    spectrum = lax.fori_loop(
        0,
        bins // dft_step,
        fill_spectrum,
        jnp.zeros((2, bins, beams, local_channels), jnp.bfloat16),
    )
    regrouped = lax.all_to_all(spectrum, "wide", split_axis=1, concat_axis=3, tiled=True)
    all_channels = regrouped.shape[3]
    fractions = delay_fractions(all_channels, all_channels)
    phase_step = math.gcd(local_bins, min(512, max(1, 2097152 // (all_channels * total_dms))))

    def fill_trials(step, buffer):
        offset = step * phase_step
        spec_part = lax.dynamic_slice_in_dim(regrouped, offset, phase_step, 1)
        cos_tab, sin_tab = phase_tables(
            position * local_bins + offset, phase_step, fractions, dm_delays, samples
        )
        block = dedisperse_block(spec_part[0], spec_part[1], cos_tab, sin_tab).astype(jnp.bfloat16)
        return lax.dynamic_update_slice_in_dim(buffer, block, offset, 0)

    dm_spectrum = lax.fori_loop(
        0,
        local_bins // phase_step,
        fill_trials,
        jnp.zeros((local_bins, 2, beams, total_dms), jnp.bfloat16),
    )
    by_trial = lax.all_to_all(dm_spectrum, "wide", split_axis=3, concat_axis=0, tiled=True)
    flat = by_trial.reshape(bins * 2, beams * local_dms)
    inverse_step = math.gcd(bins, 512)

    def add_series(step, total):
        first_bin = step * inverse_step
        part_rows = lax.dynamic_slice_in_dim(flat, first_bin * 2, inverse_step * 2, 0)
        table = inverse_tables(first_bin, inverse_step, samples, C)
        return total + lax.dot_general(
            part_rows, table, (((0,), (0,)), ((), ())), preferred_element_type=jnp.float32
        )

    series = lax.fori_loop(
        0, bins // inverse_step, add_series, jnp.zeros((beams * local_dms, samples), jnp.float32)
    )
    return series.reshape(beams, local_dms, samples)


def solution(mesh):
    return jax.shard_map(
        body,
        mesh=mesh,
        in_specs=(P("beam", "wide", None), P(("beam", "wide")), P(), P()),
        out_specs=P("beam", "wide", None),
        check_vma=False,
    )
```

profile of v0, /device:TPU:0, one launch (start us, length us, event | category | flops | bytes accessed | tf_op | source)
XLA Modules:
  0.0 588.4 jit_solution(12645496594164562645)
XLA Ops:
  0.0 0.7 convert_element_type.159
  0.7 2.1 convert_multiply_fusion
  2.8 5.7 copy.73
  8.5 0.1 convert_reduce_fusion
  8.6 2.7 reduce_sum.18
  11.3 0.4 convolution_bitcast_fusion.1
  11.7 35.2 %psum.7 = f32[1,8,8]{1,2,0:T(8,128)S(1)} all-reduce(f32[1,8,8]{1,2,0:T(8,128)S(1)} %convolution_bitcast_fusion.1), channel_id=1, replica_groups=mesh['beam'=2,'wide'=16] {'wide'}, use_global_device_ids=true, to_apply=%region_2.0 | all-reduce | flops 64 | bytes 512 | tf_op jit(solution)/shard_map/psum | solution.py:87
  47.0 0.1 fusion.61
  47.0 0.2 convolution_bitcast_fusion
  47.2 0.2 copy.55
  47.4 2.3 div.55
  49.8 4.9 div.56
  54.7 4.3 fusion.47
  59.0 1.5 broadcast_in_dim.59.clone
  60.6 97.5 %while.47 = (s32[]{:T(128)}, bf16[2,1024,1,256]{3,0,2,1:T(2,128)(2,1)}, bf16[256,4096]{1,0:T(8,128)(2,1)}, s32[]{:T(128)}, s32[]{:T(128)}, /*index=5*/s32[]{:T(128)}, s32[]{:T(128)}) while((s32[]{:T(128)}, bf16[2,1024,1,256]{3,0,2,1:T(2,128)(2,1)}, bf16[256,4096]{1,0:T(8,128)(2,1)}, s32[]{:T(128)}, s32[]{:T(128)}, /*index=5*/s32[]{:T(128)}, ...), condition=%wide.region_4.5_spmd, body=%wide.region_3.4_spmd.sunk | while | flops 2187592192 | bytes 45617308 | solution.py:109
  60.6 35.3 %cosine_convert_fusion.7 = (bf16[1,512,4096]{2,1,0:T(8,128)(2,1)S(1)}, bf16[1,512,4096]{2,1,0:T(8,128)(2,1)}) fusion(s32[512]{0:T(512)S(1)} %iota_add_fusion.7), kind=kLoop, calls=%fused_computation.9.clone.1 | loop fusion | flops 35651584 | bytes 8390656 | tf_op jit(solution)/shard_map/convert
  95.9 6.3 %pad_maximum_fusion.6 = bf16[2,512,4096]{2,1,0:T(8,128)(2,1)} fusion(bf16[1,512,4096]{2,1,0:T(8,128)(2,1)} %get-tuple-element.498, bf16[1,512,4096]{2,1,0:T(8,128)(2,1)S(1)} %get-tuple-element.499), kind=kLoop, calls=%fused_computation.7.clone.1 | loop fusion | flops 4194304 | bytes 16777216 | tf_op jit(solution)/shard_map/while/body/eval_jaxpr/stack | solution.py:31
  102.2 5.7 convolution_convert_fusion.2
  108.0 1.4 copy_dynamic-update-slice_fusion.2
  109.3 35.2 %cosine_convert_fusion.7 = (bf16[1,512,4096]{2,1,0:T(8,128)(2,1)S(1)}, bf16[1,512,4096]{2,1,0:T(8,128)(2,1)}) fusion(s32[512]{0:T(512)S(1)} %iota_add_fusion.7), kind=kLoop, calls=%fused_computation.9.clone.1 | loop fusion | flops 35651584 | bytes 8390656 | tf_op jit(solution)/shard_map/convert
  144.6 6.3 %pad_maximum_fusion.6 = bf16[2,512,4096]{2,1,0:T(8,128)(2,1)} fusion(bf16[1,512,4096]{2,1,0:T(8,128)(2,1)} %get-tuple-element.498, bf16[1,512,4096]{2,1,0:T(8,128)(2,1)S(1)} %get-tuple-element.499), kind=kLoop, calls=%fused_computation.7.clone.1 | loop fusion | flops 4194304 | bytes 16777216 | tf_op jit(solution)/shard_map/while/body/eval_jaxpr/stack | solution.py:31
  150.9 5.8 convolution_convert_fusion.2
  156.7 1.3 copy_dynamic-update-slice_fusion.2
  158.0 3.7 all-to-all-start
  161.7 22.9 %all-to-all-done = bf16[2,1024,1,256]{3,0,2,1:T(2,128)(2,1)S(1)} async-done(((bf16[2,1024,1,256]{3,0,2,1:T(2,128)(2,1)}), bf16[2,1024,1,256]{3,0,2,1:T(2,128)(2,1)S(1)}, u32[]{:S(2)}, u32[]{:S(2)}) %all-to-all-start) | async-done | bytes 1048608 | tf_op jit(solution)/shard_map/all_to_all | solution.py:115
  184.6 0.6 copy.84
  185.2 0.5 all_to_all.27
  185.7 0.6 broadcast_in_dim.58.clone
  186.3 235.6 %while.48 = (s32[]{:T(128)}, bf16[64,2,1,16]{0,1,2,3:T(2,128)(2,1)}, bf16[2,64,1,4096]{3,1,2,0:T(8,128)(2,1)S(1)}, s32[]{:T(128)}, s32[16]{0:T(128)S(1)}, /*inde...) while((s32[]{:T(128)}, bf16[64,2,1,16]{0,1,2,3:T(2,128)(2,1)}, ...), condition=%wide.region_6.7_spmd.clone, body=%wide.region_5.6_spmd.clone.sunk | while | flops 41979944 | bytes 2236923 | solution.py:129
  187.0 0.1 multiply_convert_fusion.5
  187.0 27.7 %fusion.88 = f32[32,1,16]{2,1,0:T(1,128)S(1)} fusion(f32[4096]{0:T(1024)S(1)} %add_multiply_fusion.2, f32[32,16]{1,0:T(8,128)S(1)} %multiply_convert_fusion.5, bf16[32,4096,1]{1,0,2:T(8,128)(2,1)S(1)} %get-tuple-element.506), kind=kOutput, calls=%fused_computation.20.clone.1 | convolution fusion | flops 10485760 | bytes 282624 | tf_op jit(solution)/shard_map/while/body/eval_jaxpr/fbc,fcd->fbd/dot_general | solution.py:63
  214.7 0.1 copy.102
  214.8 27.8 %fusion.89 = f32[32,1,16]{2,1,0:T(1,128)S(1)} fusion(f32[4096]{0:T(1024)S(1)} %add_multiply_fusion.2, f32[32,16]{1,0:T(8,128)S(1)} %multiply_convert_fusion.5, bf16[32,4096,1]{1,0,2:T(8,128)(2,1)S(1)} %get-tuple-element.505), kind=kOutput, calls=%fused_computation.19.clone.1 | convolution fusion | flops 10485760 | bytes 282624 | tf_op jit(solution)/shard_map/while/body/eval_jaxpr/fbc,fcd->fbd/dot_general | solution.py:68
  242.6 0.1 copy.103
  242.7 28.4 %fusion.90 = f32[32,1,16]{2,1,0:T(1,128)S(1)} fusion(f32[4096]{0:T(1024)S(1)} %add_multiply_fusion.2, f32[32,16]{1,0:T(8,128)S(1)} %multiply_convert_fusion.5, bf16[32,4096,1]{1,0,2:T(8,128)(2,1)S(1)} %get-tuple-element.506), kind=kOutput, calls=%fused_computation.21.clone.1 | convolution fusion | flops 10485760 | bytes 282624 | tf_op jit(solution)/shard_map/while/body/eval_jaxpr/fbc,fcd->fbd/dot_general | solution.py:66
  271.1 28.2 %fusion.87 = f32[32,1,16]{2,1,0:T(1,128)S(1)} fusion(f32[4096]{0:T(1024)S(1)} %add_multiply_fusion.2, f32[32,16]{1,0:T(8,128)S(1)} %multiply_convert_fusion.5, bf16[32,4096,1]{1,0,2:T(8,128)(2,1)S(1)} %get-tuple-element.505), kind=kOutput, calls=%fused_computation.22.clone.1 | convolution fusion | flops 10485760 | bytes 282624 | tf_op jit(solution)/shard_map/while/body/eval_jaxpr/fbc,fcd->fbd/dot_general | solution.py:65
  299.3 0.1 copy.101
  299.4 1.4 dynamic_update_slice.24
  301.3 0.1 multiply_convert_fusion.5
  301.4 27.7 %fusion.88 = f32[32,1,16]{2,1,0:T(1,128)S(1)} fusion(f32[4096]{0:T(1024)S(1)} %add_multiply_fusion.2, f32[32,16]{1,0:T(8,128)S(1)} %multiply_convert_fusion.5, bf16[32,4096,1]{1,0,2:T(8,128)(2,1)S(1)} %get-tuple-element.506), kind=kOutput, calls=%fused_computation.20.clone.1 | convolution fusion | flops 10485760 | bytes 282624 | tf_op jit(solution)/shard_map/while/body/eval_jaxpr/fbc,fcd->fbd/dot_general | solution.py:63
  329.0 0.1 copy.102
  329.1 27.8 %fusion.89 = f32[32,1,16]{2,1,0:T(1,128)S(1)} fusion(f32[4096]{0:T(1024)S(1)} %add_multiply_fusion.2, f32[32,16]{1,0:T(8,128)S(1)} %multiply_convert_fusion.5, bf16[32,4096,1]{1,0,2:T(8,128)(2,1)S(1)} %get-tuple-element.505), kind=kOutput, calls=%fused_computation.19.clone.1 | convolution fusion | flops 10485760 | bytes 282624 | tf_op jit(solution)/shard_map/while/body/eval_jaxpr/fbc,fcd->fbd/dot_general | solution.py:68
  356.9 0.1 copy.103
  357.0 28.4 %fusion.90 = f32[32,1,16]{2,1,0:T(1,128)S(1)} fusion(f32[4096]{0:T(1024)S(1)} %add_multiply_fusion.2, f32[32,16]{1,0:T(8,128)S(1)} %multiply_convert_fusion.5, bf16[32,4096,1]{1,0,2:T(8,128)(2,1)S(1)} %get-tuple-element.506), kind=kOutput, calls=%fused_computation.21.clone.1 | convolution fusion | flops 10485760 | bytes 282624 | tf_op jit(solution)/shard_map/while/body/eval_jaxpr/fbc,fcd->fbd/dot_general | solution.py:66
  385.4 0.1 copy.104
  385.5 28.2 %fusion.87 = f32[32,1,16]{2,1,0:T(1,128)S(1)} fusion(f32[4096]{0:T(1024)S(1)} %add_multiply_fusion.2, f32[32,16]{1,0:T(8,128)S(1)} %multiply_convert_fusion.5, bf16[32,4096,1]{1,0,2:T(8,128)(2,1)S(1)} %get-tuple-element.505), kind=kOutput, calls=%fused_computation.22.clone.1 | convolution fusion | flops 10485760 | bytes 282624 | tf_op jit(solution)/shard_map/while/body/eval_jaxpr/fbc,fcd->fbd/dot_general | solution.py:65
  413.6 0.1 copy.101
  413.8 3.1 dynamic_update_slice.24
  421.9 6.8 %all-to-all-start.1 = ((bf16[64,2,1,16]{0,1,2,3:T(2,128)(2,1)}), bf16[64,2,1,16]{0,1,2,3:T(2,128)(2,1)S(1)}, u32[]{:S(2)}, u32[]{:S(2)}) async-start(bf16[64,2,1,16]{0,1,2,3:T(2,128)(2,1)} %get-tuple-element.334), calls=%async_computation.1 | async-start | bytes 16384 | tf_op jit(solution)/shard_map/all_to_all | solution.py:135
  428.8 6.3 %all-to-all-done.1 = bf16[64,2,1,16]{0,1,2,3:T(2,128)(2,1)S(1)} async-done(((bf16[64,2,1,16]{0,1,2,3:T(2,128)(2,1)}), bf16[64,2,1,16]{0,1,2,3:T(2,128)(2,1)S(1)}, u32[]{:S(2)}, u32[]{:S(2)}) %all-to-all-start.1) | async-done | bytes 4128 | tf_op jit(solution)/shard_map/all_to_all | solution.py:135
  435.1 0.2 copy.68
  435.3 0.3 reshape.489
  435.6 152.0 %while.49 = (s32[]{:T(128)}, f32[1,4096]{1,0:T(1,128)S(1)}, bf16[2048,1]{0,1:T(2,128)(2,1)S(1)}, s32[]{:T(128)}, s32[]{:T(128)}, /*index=5*/s32[]{:T(128)}, s32[]{:T(128)}, s32[]{:T(128)}) while((s32[]{:T(128)}, f32[1,4096]{1,0:T(1,128)S(1)}, bf16[2048,1]{0,1:T(2,128)(2,1)S(1)}, s32[]{:T(128)}, s32[]{:T(128)}, ...), condition=%wide.region_8.9_spmd.clone, body=%wide.region_7.8_spmd.clone.sunk | while | flops 50342912 | bytes 67158176 | solution.py:147
  435.7 35.7 %multiply_convert_fusion.6 = (bf16[512,1,4096]{2,0,1:T(8,128)(2,1)S(1)}, bf16[512,1,4096]{2,0,1:T(8,128)(2,1)}) fusion(s32[512]{0:T(512)S(1)} %iota_add_fusion.9, f32[512]{0:T(512)S(1)} %get-tuple-element.512, f32[512]{0:T(512)S(1)} %get-tuple-element.513), kind=kLoop, calls=%fused_computation.63.clone.1 | loop fusion | flops 37748736 | bytes 8394752 | tf_op jit(solution)/shard_map/convert.6
  471.3 6.2 %pad_maximum_fusion.8 = bf16[512,2,4096]{2,0,1:T(8,128)(2,1)} fusion(bf16[512,1,4096]{2,0,1:T(8,128)(2,1)} %get-tuple-element.514, bf16[512,1,4096]{2,0,1:T(8,128)(2,1)S(1)} %get-tuple-element.515), kind=kLoop, calls=%fused_computation.61.clone.1 | loop fusion | flops 4194304 | bytes 16777216 | tf_op jit(solution)/shard_map/while/body/eval_jaxpr/stack | solution.py:41
  477.5 16.4 %copy.106 = bf16[512,2,4096]{2,1,0:T(2,128)(2,1)} copy(bf16[512,2,4096]{2,0,1:T(8,128)(2,1)} %pad_maximum_fusion.8) | data formatting | bytes 16777216 | tf_op jit(solution)/shard_map/while/body/eval_jaxpr/stack | solution.py:41
  493.9 13.1 %convert_element_type.227 = bf16[1024,4096]{1,0:T(8,128)(2,1)} reshape(bf16[512,2,4096]{2,1,0:T(2,128)(2,1)} %copy.106) | data formatting | bytes 16777216 | tf_op jit(solution)/shard_map/while/body/eval_jaxpr/convert_element_type | solution.py:44
  507.0 4.6 convolution_add_fusion.2
  511.6 35.7 %multiply_convert_fusion.6 = (bf16[512,1,4096]{2,0,1:T(8,128)(2,1)S(1)}, bf16[512,1,4096]{2,0,1:T(8,128)(2,1)}) fusion(s32[512]{0:T(512)S(1)} %iota_add_fusion.9, f32[512]{0:T(512)S(1)} %get-tuple-element.512, f32[512]{0:T(512)S(1)} %get-tuple-element.513), kind=kLoop, calls=%fused_computation.63.clone.1 | loop fusion | flops 37748736 | bytes 8394752 | tf_op jit(solution)/shard_map/convert.6
  547.3 6.2 %pad_maximum_fusion.8 = bf16[512,2,4096]{2,0,1:T(8,128)(2,1)} fusion(bf16[512,1,4096]{2,0,1:T(8,128)(2,1)} %get-tuple-element.514, bf16[512,1,4096]{2,0,1:T(8,128)(2,1)S(1)} %get-tuple-element.515), kind=kLoop, calls=%fused_computation.61.clone.1 | loop fusion | flops 4194304 | bytes 16777216 | tf_op jit(solution)/shard_map/while/body/eval_jaxpr/stack | solution.py:41
  553.5 16.4 %copy.106 = bf16[512,2,4096]{2,1,0:T(2,128)(2,1)} copy(bf16[512,2,4096]{2,0,1:T(8,128)(2,1)} %pad_maximum_fusion.8) | data formatting | bytes 16777216 | tf_op jit(solution)/shard_map/while/body/eval_jaxpr/stack | solution.py:41
  569.9 13.1 %convert_element_type.227 = bf16[1024,4096]{1,0:T(8,128)(2,1)} reshape(bf16[512,2,4096]{2,1,0:T(2,128)(2,1)} %copy.106) | data formatting | bytes 16777216 | tf_op jit(solution)/shard_map/while/body/eval_jaxpr/convert_element_type | solution.py:44
  583.0 4.6 convolution_add_fusion.2
  587.6 0.6 copy-done.2
  (32 shorter events, 0.3 us)
Async XLA Ops:
  0.0 8.5 %copy-start.4 = (s32[7]{0:T(128)S(1)}, s32[7]{0:T(128)}, u32[]{:S(2)}) copy-start(s32[7]{0:T(128)} %param.12) | copy-start | bytes 88
  8.6 46.1 %copy-start = (bf16[1,256,4096]{2,1,0:T(8,128)(2,1)S(1)}, bf16[1,256,4096]{2,1,0:T(8,128)(2,1)}, u32[]{:S(2)}) copy-start(bf16[1,256,4096]{2,1,0:T(8,128)(2,1)} %param.10) | copy-start | bytes 6291460
  60.6 125.8 %copy-start.3 = (s32[16]{0:T(128)S(1)}, s32[16]{0:T(128)}, u32[]{:S(2)}) copy-start(s32[16]{0:T(128)} %param.13) | copy-start | bytes 196
  95.9 6.3 %copy-start.1 = (bf16[256,4096]{1,0:T(8,128)(2,1)S(1)}, bf16[256,4096]{1,0:T(8,128)(2,1)}, u32[]{:S(2)}) copy-start(bf16[256,4096]{1,0:T(8,128)(2,1)} %get-tuple-element.532) | copy-start | bytes 6291460 | tf_op jit(solution)/shard_map/while
  144.6 6.3 %copy-start.1 = (bf16[256,4096]{1,0:T(8,128)(2,1)S(1)}, bf16[256,4096]{1,0:T(8,128)(2,1)}, u32[]{:S(2)}) copy-start(bf16[256,4096]{1,0:T(8,128)(2,1)} %get-tuple-element.532) | copy-start | bytes 6291460 | tf_op jit(solution)/shard_map/while
  158.0 26.6 %all-to-all-start = ((bf16[2,1024,1,256]{3,0,2,1:T(2,128)(2,1)}), bf16[2,1024,1,256]{3,0,2,1:T(2,128)(2,1)S(1)}, u32[]{:S(2)}, u32[]{:S(2)}) async-start(bf16[2,1024,1,256]{3,0,2,1:T(2,128)(2,1)} %get-tuple-element.333), calls=%async_computation | async-start | bytes 2097152 | tf_op jit(solution)/shard_map/all_to_all | solution.py:115
  421.9 13.2 %all-to-all-start.1 = ((bf16[64,2,1,16]{0,1,2,3:T(2,128)(2,1)}), bf16[64,2,1,16]{0,1,2,3:T(2,128)(2,1)S(1)}, u32[]{:S(2)}, u32[]{:S(2)}) async-start(bf16[64,2,1,16]{0,1,2,3:T(2,128)(2,1)} %get-tuple-element.334), calls=%async_computation.1 | async-start | bytes 16384 | tf_op jit(solution)/shard_map/all_to_all | solution.py:135
  587.6 0.6 copy-start.2
where the time goes:
time: 594 us; the launch traced here: 588 us
  matrix products  245 us (41%)
  other arithmetic  177 us (30%)
  local copies, waits for them, and re-layouts  84.5 us (14%)
  blocking collectives  35.2 us (6%)
  waiting for transfers between devices  29.2 us (5%)
  starting transfers between devices  10.5 us (2%)
  loops' own time  6.19 us (1%)
    another operation x4, other arithmetic  142 us
    dot_general x2, matrix products, dedisperse_block(): jnp.einsum('fbc,fcd->fbd', spec_real, sin_tab, preferred_element_type=jnp...  56.8 us
    dot_general x2, matrix products, dedisperse_block(): jnp.einsum('fbc,fcd->fbd', spec_imag, sin_tab, preferred_element_type=jnp...  56.3 us
    dot_general x2, matrix products, dedisperse_block(): jnp.einsum('fbc,fcd->fbd', spec_imag, cos_tab, preferred_element_type=jnp...  55.6 us
    dot_general x2, matrix products, dedisperse_block(): jnp.einsum('fbc,fcd->fbd', spec_real, cos_tab, preferred_element_type=jnp...  55.3 us
    psum x1, blocking collectives, body(): band_power = lax.psum(local_power, 'wide')  35.2 us
    another operation x2, local copies, waits for them, and re-layouts, inverse_tables(): jnp.stack([weight[:, None] * jnp.cos(angle), -weight[:, None] * jnp.sin(a...  32.8 us
    convert_element_type x2, local copies, waits for them, and re-layouts, inverse_tables(): return tables.reshape(2 * bin_count, samples).astype(jnp.bfloat16)  26.3 us
  transfers between devices with their start and end apart: 2, of which 2 were waited for; matrix products, arithmetic and copies ran while one was open for 0% of the time, Pallas kernels for 0%

commit v1 on v0

v1 whole, which is shorter than its diff:
```python
import functools
import math

import jax
import jax.numpy as jnp
import ml_dtypes
import numpy as np
from jax import lax
from jax.experimental import pallas as pl
from jax.experimental.pallas import tpu as pltpu
from jax.sharding import PartitionSpec as P

NBLK = 8
F32 = jnp.float32
BF16 = jnp.bfloat16
VMEM = pl.BlockSpec(memory_space=pltpu.VMEM)
SMEM = pl.BlockSpec(memory_space=pltpu.SMEM)
VMEM_BYTES = 48 * 2**20


def trig_coefficients(terms):
    n = 400
    y = 0.125 + 0.125 * np.cos(np.pi * (np.arange(n) + 0.5) / n)
    x = np.sqrt(y)
    out = []
    for values in (np.cos(2 * np.pi * x), np.sin(2 * np.pi * x) / x):
        fit = np.polynomial.Chebyshev.fit(y, values, terms - 1, domain=[0.0, 0.25])
        out.append([float(v) for v in fit.convert(kind=np.polynomial.Polynomial).coef])
    return out


def cos_sin_cycles(x):
    cos_c, sin_c = trig_coefficients(9)
    x = x - jnp.round(x)
    y = x * x
    c = jnp.full_like(x, cos_c[-1])
    s = jnp.full_like(x, sin_c[-1])
    for a, b in zip(cos_c[-2::-1], sin_c[-2::-1]):
        c = c * y + a
        s = s * y + b
    return c, s * x


def class_bins(r, bins):
    b = np.arange(bins // 64)[:, None]
    i = (np.arange(8)[None, :] - r) % 8
    return 64 * b + 8 * i + r


def forward_tables(samples):
    bins = samples // 4
    u = np.arange(samples // NBLK)

    def rows(r):
        f = class_bins(r, bins)[:, :, None]
        angle = 2.0 * np.pi * ((f * u) % samples) / samples
        return np.cos(angle), np.sin(angle)

    def put(real, imag):
        return np.stack([real, imag], axis=1).reshape(2 * bins // 8, -1)

    real_classes = []
    for r in (0, 4):
        c, s = rows(r)
        real_classes.append(put(c, -s))
    pairs = []
    for r in (1, 2, 3):
        c, s = rows(r)
        first = put(np.concatenate([c, s], -1), np.concatenate([-s, c], -1))
        c, s = rows(8 - r)
        second = put(np.concatenate([c, -s], -1), np.concatenate([-s, -c], -1))
        pairs.append(np.concatenate([first, second], 0))
    return (
        np.stack(real_classes).astype(ml_dtypes.bfloat16),
        np.stack(pairs).astype(ml_dtypes.bfloat16),
    )


def inverse_tables(samples, channels):
    bins = samples // 4
    g = np.arange(bins // 8)[:, None]
    q = np.arange(samples // 8)[None, :]
    angle = 2.0 * np.pi * ((8 * g * q) % samples) / samples
    first = np.concatenate([np.cos(angle), np.sin(angle)], 1).astype(ml_dtypes.bfloat16)
    r = np.arange(8)[:, None]
    weight = 2.0 / (samples * math.sqrt(channels))
    angle = 2.0 * np.pi * r * q / samples
    twiddle = (weight * np.stack([np.cos(angle), np.sin(angle)])).astype(np.float32)
    p = np.arange(8)[:, None]
    angle = 2.0 * np.pi * ((p * r.T) % 8) / 8
    last = np.concatenate([np.cos(angle), -np.sin(angle)], 1).astype(np.float32)
    return first, twiddle, last


def band_place(edges_ref, first, channels):
    band = jnp.int32(0)
    cut = jnp.int32(channels)
    for e in range(edges_ref.shape[0]):
        edge = edges_ref[e]
        band = band + (edge <= first).astype(jnp.int32)
        cut = jnp.where(edge > first, jnp.minimum(cut, edge), cut)
    return band, cut


def power_kernel(group, edges_ref, keep_ref, x_ref, out_ref, mask_ref):
    local = x_ref.shape[0]
    window = x_ref.shape[1] // NBLK
    first = lax.axis_index("wide") * local
    band, cut = band_place(edges_ref, first, local * group)
    ids = first + lax.broadcasted_iota(jnp.int32, (1, local), 1)
    keep = keep_ref[...].astype(F32)
    masks = []
    for j in range(2):
        inside = (ids < cut) if j == 0 else (ids >= cut)
        row = jnp.where(inside, keep, 0.0)
        column = jnp.broadcast_to(row, (128, local)).T
        mask_ref[j] = column
        masks.append(column)
    rows = []
    for k in range(NBLK):
        totals = [jnp.zeros((16, 128), F32) for _ in range(2)]
        for c in range(0, local, 16):
            squares = jnp.zeros((16, 128), F32)
            for u in range(k * window, (k + 1) * window, 128):
                v = x_ref[c : c + 16, u : u + 128].astype(F32)
                squares = squares + v * v
            for j in range(2):
                totals[j] = totals[j] + squares * mask_ref[j, c : c + 16, :]
        rows.append(totals)
    flat = jnp.concatenate(
        [jnp.sum(rows[k][j], axis=0, keepdims=True) for j in range(2) for k in range(NBLK)], axis=0
    )
    sums = jnp.sum(flat, axis=1, keepdims=True) * (1.0 / window)
    lanes = out_ref.shape[1]
    lane = lax.broadcasted_iota(jnp.int32, (2 * NBLK, lanes), 1)
    row = lax.broadcasted_iota(jnp.int32, (2 * NBLK, lanes), 0)
    placed = jnp.where(lane == band * NBLK + row, jnp.broadcast_to(sums, lane.shape), 0.0)
    out_ref[...] = jnp.broadcast_to(jnp.sum(placed, axis=0, keepdims=True), out_ref.shape)


def phase_kernel(channels, samples, delays_ref, base_ref, turn_ref, step_ref):
    local, lanes = base_ref.shape[1:]
    first = lax.axis_index("wide") * local
    lane = lax.broadcasted_iota(jnp.int32, (8, lanes), 1)
    delay = jnp.zeros((8, lanes), F32)
    for d in range(delays_ref.shape[0]):
        delay = jnp.where((lane >> 3) == d, delays_ref[d].astype(F32), delay)
    start = (3.5 + 8.0 * (lane & 7).astype(F32)) * delay

    def rows(n, carry):
        c = pl.multiple_of(n * 8, 8)
        channel = first + c + lax.broadcasted_iota(jnp.int32, (8, lanes), 0)
        ratio = 0.5 + 0.5 * (channel.astype(F32) + 0.5) / channels
        fraction = (1.0 / (ratio * ratio) - 1.0) / 3.0 / samples
        at = pl.ds(c, 8)
        base_ref[0, at, :], base_ref[1, at, :] = cos_sin_cycles(start * fraction)
        turn_ref[0, at, :], turn_ref[1, at, :] = cos_sin_cycles((64.0 * delay) * fraction)
        for j in range(4):
            step_ref[j, 0, at, :], step_ref[j, 1, at, :] = cos_sin_cycles(((j + 0.5) * delay) * fraction)
        return carry

    lax.fori_loop(0, local // 8, rows, 0, unroll=2)


def window_classes(y):
    half = math.sqrt(0.5)
    e = [y[k] + y[k + 4] for k in range(4)]
    o = [y[k] - y[k + 4] for k in range(4)]
    a, b = e[0] + e[2], e[1] + e[3]
    p, q = half * (o[1] - o[3]), half * (o[1] + o[3])
    return [a + b, a - b, o[0] + p, -(o[2] + q), e[0] - e[2], e[3] - e[1], o[0] - p, o[2] - q]


def main_kernel(
    group, edges_ref, x_ref, power_ref, mask_ref, base_ref, turn_ref, step_ref, real_ref, pair_ref,
    out_ref, z_ref, spec_ref, even_ref, odd_ref, state_ref, part_ref,
):
    local, samples = x_ref.shape
    window = samples // NBLK
    lanes = base_ref.shape[2]
    first = lax.axis_index("wide") * local
    channels = local * group
    band, _ = band_place(edges_ref, first, channels)

    power = jnp.sum(power_ref[...], axis=0, keepdims=True)
    wide = power.shape[1]
    lane = lax.broadcasted_iota(jnp.int32, (1, wide), 1)
    width = jnp.ones((1, wide), F32)
    edges = edges_ref.shape[0]
    for j in range(edges + 1):
        low = edges_ref[j - 1] if j else jnp.int32(0)
        high = edges_ref[j] if j < edges else jnp.int32(channels)
        width = jnp.where((lane >> 3) == j, (high - low).astype(F32), width)
    floor = jnp.sqrt(power / width + 1e-05)
    inverse = jnp.broadcast_to(1.0 / floor, (8, wide))
    inverse = pltpu.roll(inverse, (wide - band * NBLK) % wide, 1)
    scale = [
        [jnp.broadcast_to(inverse[:, j * NBLK + k : j * NBLK + k + 1], (8, 128)) for k in range(NBLK)]
        for j in range(2)
    ]
    scale = [[jnp.concatenate([v, v], axis=0) for v in row] for row in scale]

    def combine(n, carry):
        c = pl.ds(pl.multiple_of(n * 16, 16), 16)
        m0, m1 = mask_ref[0, c, :], mask_ref[1, c, :]
        weight = [m0 * scale[0][k] + m1 * scale[1][k] for k in range(NBLK)]
        for u in range(0, window, 128):
            y = [x_ref[c, k * window + u : k * window + u + 128].astype(F32) * weight[k] for k in range(NBLK)]
            for n_out, z in enumerate(window_classes(y)):
                z_ref[c, n_out * window + u : n_out * window + u + 128] = z.astype(BF16)
        return carry

    lax.fori_loop(0, local // 16, combine, 0, unroll=2)

    rows = spec_ref.shape[1]
    contract = (((1,), (1,)), ((), ()))
    for n, r in enumerate((0, 4)):
        spec_ref[r] = lax.dot_general(
            real_ref[n], z_ref[:, n * window : (n + 1) * window], contract, preferred_element_type=F32
        ).astype(BF16)
    for n in range(3):
        z = z_ref[:, 2 * (n + 1) * window : 2 * (n + 2) * window]
        for r, at in ((n + 1, 0), (7 - n, rows)):
            spec_ref[r] = lax.dot_general(
                pair_ref[n, at : at + rows, :], z, contract, preferred_element_type=F32
            ).astype(BF16)

    sub = lax.broadcasted_iota(jnp.int32, (8, lanes), 0)
    inner = lax.broadcasted_iota(jnp.int32, (8, lanes), 1) & 7
    skew = (sub - inner) & 7
    state_ref[...] = base_ref[...]

    def phases(e_ref):
        for c in range(0, local, 16):
            at = slice(c, c + 16)
            cos0, sin0 = state_ref[0, at, :], state_ref[1, at, :]
            for j in range(4):
                cos_j, sin_j = step_ref[j, 0, at, :], step_ref[j, 1, at, :]
                cc, ss, sc, cs = cos0 * cos_j, sin0 * sin_j, sin0 * cos_j, cos0 * sin_j
                e_ref[4 + j, at, :lanes] = (cc - ss).astype(BF16)
                e_ref[4 + j, at, lanes:] = (sc + cs).astype(BF16)
                e_ref[3 - j, at, :lanes] = (cc + ss).astype(BF16)
                e_ref[3 - j, at, lanes:] = (sc - cs).astype(BF16)
            cos_t, sin_t = turn_ref[0, at, :], turn_ref[1, at, :]
            state_ref[0, at, :] = cos0 * cos_t - sin0 * sin_t
            state_ref[1, at, :] = sin0 * cos_t + cos0 * sin_t

    def dedisperse(b, e_ref):
        at = pl.ds(pl.multiple_of(b * 16, 16), 16)
        real = imag = None
        for r in range(8):
            o = jnp.dot(spec_ref[r, at, :], e_ref[r], preferred_element_type=F32)
            re = o[0:8, :lanes] - o[8:16, lanes:]
            im = o[0:8, lanes:] + o[8:16, :lanes]
            real = re if r == 0 else jnp.where(skew == r, re, real)
            imag = im if r == 0 else jnp.where(skew == r, im, imag)
        for bit in (1, 2, 4):
            move = (inner & bit) != 0
            real = jnp.where(move, pltpu.roll(real, 8 - bit, 0), real)
            imag = jnp.where(move, pltpu.roll(imag, 8 - bit, 0), imag)
        part_ref[0, b] = real
        part_ref[1, b] = imag

    phases(even_ref)

    def pair(n, carry):
        phases(odd_ref)
        dedisperse(2 * n, even_ref)
        phases(even_ref)
        dedisperse(2 * n + 1, odd_ref)
        return carry

    blocks = part_ref.shape[1]
    lax.fori_loop(0, blocks // 2, pair, 0)

    block = lax.broadcasted_iota(jnp.int32, (8, 128), 1) >> 3
    for half in range(lanes // 128):
        done = []
        for part in range(2):
            v = [part_ref[part, b, :, half * 128 : half * 128 + 128] for b in range(16)]
            for bit in (1, 2, 4, 8):
                w = list(v)
                high = (block & bit) != 0
                for b in range(16):
                    if b & bit:
                        w[b] = jnp.where(high, v[b], pltpu.roll(v[b ^ bit], 128 - 8 * bit, 1))
                    else:
                        w[b] = jnp.where(high, pltpu.roll(v[b ^ bit], 8 * bit, 1), v[b])
                v = w
            done.append(v)
        for d in range(16):
            out_ref[half * 16 + d] = jnp.concatenate([done[0][d], done[1][d]], axis=0).astype(BF16)


def inverse_kernel(group, got_ref, first_ref, twiddle_ref, last_ref, out_ref):
    step = first_ref.shape[1] // 2
    trials = out_ref.shape[1]
    row = lax.broadcasted_iota(jnp.int32, (16, 128), 0)
    lane = lax.broadcasted_iota(jnp.int32, (16, 128), 1)
    dc = ((row & 7) == 0) & (lane == 0)
    for d in range(trials):
        total = got_ref[d].astype(F32)
        for n in range(1, group):
            total = total + got_ref[n * trials + d].astype(F32)
        total = jnp.where(dc, 0.5 * total, total).astype(BF16)
        y = jnp.dot(total, first_ref[...], preferred_element_type=F32)
        real = y[0:8, :step] - y[8:16, step:]
        imag = y[0:8, step:] + y[8:16, :step]
        cos, sin = twiddle_ref[0], twiddle_ref[1]
        z = jnp.concatenate([real * cos - imag * sin, real * sin + imag * cos], axis=0)
        series = jnp.dot(last_ref[...], z, precision=lax.Precision.HIGHEST, preferred_element_type=F32)
        for p in range(8):
            out_ref[0, d : d + 1, p * step : (p + 1) * step] = series[p : p + 1, :]


def call(kernel, out_shape, in_specs, scratch=(), name=None):
    return pl.pallas_call(
        kernel,
        out_shape=out_shape,
        in_specs=in_specs,
        out_specs=jax.tree.map(lambda _: VMEM, out_shape),
        scratch_shapes=list(scratch),
        compiler_params=pltpu.CompilerParams(vmem_limit_bytes=VMEM_BYTES),
        name=name,
    )


def body(filterbank, channel_mask, band_edges, dm_delays):
    _, local, samples = filterbank.shape
    group = lax.axis_size("wide")
    channels = local * group
    trials = dm_delays.shape[0]
    lanes = 8 * trials
    bins = samples // 4
    blocks = bins // 64
    shape = jax.ShapeDtypeStruct
    x = filterbank.reshape(local, samples)
    power_lanes = -(-(band_edges.shape[0] + 1) * NBLK // 128) * 128

    power, masks = call(
        functools.partial(power_kernel, group),
        (shape((group, power_lanes), F32), shape((2, local, 128), F32)),
        [SMEM, VMEM, VMEM],
        name="band_power",
    )(band_edges, channel_mask.reshape(1, local), x)
    all_power = lax.all_to_all(power, "wide", 0, 0, tiled=True)

    base, turn, step = call(
        functools.partial(phase_kernel, channels, samples),
        (shape((2, local, lanes), F32), shape((2, local, lanes), F32), shape((4, 2, local, lanes), F32)),
        [SMEM],
        name="phase_steps",
    )(dm_delays)

    real_table, pair_table = forward_tables(samples)
    partial = call(
        functools.partial(main_kernel, group),
        shape((trials, 16, 128), BF16),
        [SMEM] + [VMEM] * 8,
        [
            pltpu.VMEM((local, samples), BF16),
            pltpu.VMEM((8, bins // 4, local), BF16),
            pltpu.VMEM((8, local, 2 * lanes), BF16),
            pltpu.VMEM((8, local, 2 * lanes), BF16),
            pltpu.VMEM((2, local, lanes), F32),
            pltpu.VMEM((2, blocks, 8, lanes), F32),
        ],
        name="dedisperse",
    )(band_edges, x, all_power, masks, base, turn, step, jnp.asarray(real_table), jnp.asarray(pair_table))
    got = lax.all_to_all(partial, "wide", 0, 0, tiled=True)

    first, twiddle, last = inverse_tables(samples, channels)
    return call(
        functools.partial(inverse_kernel, group),
        shape((1, trials // group, samples), F32),
        [VMEM] * 4,
        name="inverse",
    )(got, jnp.asarray(first), jnp.asarray(twiddle), jnp.asarray(last))


def solution(mesh):
    return jax.shard_map(
        body,
        mesh=mesh,
        in_specs=(P("beam", "wide", None), P(("beam", "wide")), P(), P()),
        out_specs=P("beam", "wide", None),
        check_vma=False,
    )
```

time: 594 us -> 45.9 us (0.08)
  matrix products: 245 us -> 0 us
  other arithmetic: 177 us -> 0 us
  local copies, waits for them, and re-layouts: 84.5 us -> 8.55 us
  waiting for transfers between devices: 29.2 us -> 2.39 us
  blocking collectives: 35.2 us -> 10.3 us
  Pallas kernels: 0 us -> 16.8 us
  loops' own time: 6.19 us -> 0 us
    dot_general x14 -> x0, matrix products: 245 us -> none  [the longest x2 56.8 us: dedisperse_block(): jnp.einsum('fbc,fcd->fbd', spec_real, sin_tab, preferred_element_type=jnp...]
    another operation x12 -> x0, other arithmetic: 167 us -> none
    psum x1 -> x0, blocking collectives: 35.2 us -> none  [body(): band_power = lax.psum(local_power, 'wide')]
    another operation x4 -> x0, local copies, waits for them, and re-layouts: 32.9 us -> none  [the longest x2 32.8 us: inverse_tables(): jnp.stack([weight[:, None] * jnp.cos(angle), -weight[:, None] * jnp.sin(a...]
    all_to_all x2 -> x1, waiting for transfers between devices: 29.2 us -> 2.39 us  [body(): all_power = lax.all_to_all(power, 'wide', 0, 0, tiled=True)]
    convert_element_type x2 -> x0, local copies, waits for them, and re-layouts: 26.3 us -> none  [inverse_tables(): return tables.reshape(2 * bin_count, samples).astype(jnp.bfloat16)]
    pallas_call x0 -> x4, Pallas kernels: none -> 16.8 us  [the longest x1 12.2 us: body(): call(functools.partial(main_kernel, group), shape((trials, 16, 128), BF16...]
    all_to_all x0 -> x1, blocking collectives: none -> 10.3 us  [body(): got = lax.all_to_all(partial, 'wide', 0, 0, tiled=True)]
  transfers between devices with their start and end apart: 2 -> 1, of which waited for: 2 -> 1; matrix products, arithmetic and copies ran while one was open for 0% -> 0% of each run, Pallas kernels for 0% -> 4%
where the time goes in v1:
time: 45.9 us; the launch traced here: 45.5 us
  Pallas kernels  16.8 us (37%)
  blocking collectives  10.3 us (22%)
  local copies, waits for them, and re-layouts  8.55 us (19%)
  starting transfers between devices  7.39 us (16%)
  waiting for transfers between devices  2.39 us (5%)
    pallas_call x1, Pallas kernels, body(): call(functools.partial(main_kernel, group), shape((trials, 16, 128), BF16...  12.2 us
    all_to_all x1, blocking collectives, body(): got = lax.all_to_all(partial, 'wide', 0, 0, tiled=True)  10.3 us
    unnamed x28, local copies, waits for them, and re-layouts  8.55 us
    all_to_all x1, starting transfers between devices, body(): all_power = lax.all_to_all(power, 'wide', 0, 0, tiled=True)  7.39 us
    all_to_all x1, waiting for transfers between devices, body(): all_power = lax.all_to_all(power, 'wide', 0, 0, tiled=True)  2.39 us
    pallas_call x1, Pallas kernels, body(): call(functools.partial(phase_kernel, channels, samples), (shape((2, local...  1.9 us
    pallas_call x1, Pallas kernels, body(): call(functools.partial(power_kernel, group), (shape((group, power_lanes),...  1.78 us
    pallas_call x1, Pallas kernels, body(): call(functools.partial(inverse_kernel, group), shape((1, trials // group,...  0.92 us
  transfers between devices with their start and end apart: 1, of which 1 were waited for; matrix products, arithmetic and copies ran while one was open for 0% of the time, Pallas kernels for 4%

profile of v1, /device:TPU:0, one launch (start us, length us, event | category | flops | bytes accessed | tf_op | source)
XLA Modules:
  0.0 45.5 jit_solution(4137940821416964838)
XLA Ops:
  0.0 0.0 copy-start
  0.0 1.6 %copy-done = bf16[1,256,4096]{2,1,0:T(8,128)(2,1)S(1)} copy-done((bf16[1,256,4096]{2,1,0:T(8,128)(2,1)S(1)}, bf16[1,256,4096]{2,1,0:T(8,128)(2,1)}, u32[]{:S(2)}) %copy-start) | copy-done | bytes 2097176
  1.6 0.0 copy-start.10
  1.6 0.7 %copy-done.10 = s32[7]{0:T(128)S(1)} copy-done((s32[7]{0:T(128)S(1)}, s32[7]{0:T(128)}, u32[]{:S(2)}) %copy-start.10) | copy-done | bytes 52
  2.2 0.0 copy-start.12
  2.2 0.7 %copy-done.12 = s32[256]{0:T(256)S(1)} copy-done((s32[256]{0:T(256)S(1)}, s32[256]{0:T(256)}, u32[]{:S(2)}) %copy-start.12) | copy-done | bytes 1048
  2.9 0.0 copy-start.1
  2.9 1.8 %band_power.1 = (f32[16,128]{1,0:T(8,128)}, f32[2,256,128]{2,1,0:T(8,128)S(1)}) custom-call(s32[7]{0:T(128)S(1)} %copy-done.10, s32[1,256]{1,0:T(1,128)S(1)} %bitcast.9, bf16[256,4096]{1,0:T(8,128)(2,1)S(1)} %bitcast.6), custom_call_target="tpu_custom_call" | custom-call | tf_op jit(solution)/shard_map/band_power/pallas_call | solution.py:340
  4.7 7.4 %all-to-all-start = ((f32[16,1,128]{2,1,0:T(1,128)}), f32[16,1,128]{2,1,0:T(1,128)S(1)}, u32[]{:S(2)}, u32[]{:S(2)}) async-start(f32[16,1,128]{2,1,0:T(1,128)} %bitcast.3), calls=%async_computation | async-start | bytes 16384 | tf_op jit(solution)/shard_map/all_to_all | solution.py:346
  12.1 0.0 copy-start.13
  12.1 0.6 %copy-done.13 = s32[16]{0:T(128)S(1)} copy-done((s32[16]{0:T(128)S(1)}, s32[16]{0:T(128)}, u32[]{:S(2)}) %copy-start.13) | copy-done | bytes 88
  12.8 1.9 %phase_steps.1 = (f32[2,256,128]{2,1,0:T(8,128)S(1)}, f32[2,256,128]{2,1,0:T(8,128)S(1)}, f32[4,2,256,128]{3,2,1,0:T(8,128)S(1)}) custom-call(s32[16]{0:T(128)S(1)} %copy-done.13), custom_call_target="tpu_custom_call" | custom-call | tf_op jit(solution)/shard_map/phase_steps/pallas_call | solution.py:348
  14.7 0.0 copy-start.3
  14.7 0.7 %copy-done.3 = f32[2,256,128]{2,1,0:T(8,128)} copy-done((f32[2,256,128]{2,1,0:T(8,128)}, f32[2,256,128]{2,1,0:T(8,128)S(1)}, u32[]{:S(2)}) %copy-start.3) | copy-done | bytes 262168
  15.4 0.0 copy-start.5
  15.4 0.7 %copy-done.5 = f32[2,256,128]{2,1,0:T(8,128)} copy-done((f32[2,256,128]{2,1,0:T(8,128)}, f32[2,256,128]{2,1,0:T(8,128)S(1)}, u32[]{:S(2)}) %copy-start.5) | copy-done | bytes 262168
  16.0 2.4 %all-to-all-done = f32[16,1,128]{2,1,0:T(1,128)S(1)} async-done(((f32[16,1,128]{2,1,0:T(1,128)}), f32[16,1,128]{2,1,0:T(1,128)S(1)}, u32[]{:S(2)}, u32[]{:S(2)}) %all-to-all-start) | async-done | bytes 8224 | tf_op jit(solution)/shard_map/all_to_all | solution.py:346
  18.4 0.0 copy-done.1
  18.4 0.0 copy-start.2
  18.4 1.0 %copy-done.2 = bf16[2,256,512]{2,1,0:T(8,128)(2,1)S(1)} copy-done((bf16[2,256,512]{2,1,0:T(8,128)(2,1)S(1)}, bf16[2,256,512]{2,1,0:T(8,128)(2,1)}, u32[]{:S(2)}) %copy-start.2) | copy-done | bytes 524312
  19.5 0.0 copy-start.4
  19.5 0.9 %copy-done.4 = f32[2,256,128]{2,1,0:T(8,128)S(1)} copy-done((f32[2,256,128]{2,1,0:T(8,128)S(1)}, f32[2,256,128]{2,1,0:T(8,128)}, u32[]{:S(2)}) %copy-start.4) | copy-done | bytes 262168
  20.4 0.0 copy-start.6
  20.4 0.9 %copy-done.6 = f32[2,256,128]{2,1,0:T(8,128)S(1)} copy-done((f32[2,256,128]{2,1,0:T(8,128)S(1)}, f32[2,256,128]{2,1,0:T(8,128)}, u32[]{:S(2)}) %copy-start.6) | copy-done | bytes 262168
  21.4 0.0 copy-start.11
  21.4 0.7 %copy-done.11 = s32[7]{0:T(128)S(1)} copy-done((s32[7]{0:T(128)S(1)}, s32[7]{0:T(128)}, u32[]{:S(2)}) %copy-start.11) | copy-done | bytes 52
  22.0 0.0 copy-start.7
  22.0 0.0 copy-start.8
  22.0 0.0 copy-start.9
  22.0 12.2 %dedisperse.1 = bf16[16,16,128]{2,1,0:T(8,128)(2,1)S(1)} custom-call(s32[7]{0:T(128)S(1)} %copy-done.11, bf16[256,4096]{1,0:T(8,128)(2,1)S(1)} %bitcast.7, f32[16,128]{1,0:T(8,128)S(1)} %bitcast.8, f32[2,256,128]{2,1,0:T(8,128)S(1)} %get-tuple-element.11.mask_ref, f32[2,256,128]{2,1,0:T(8,128)S(1)} %copy-done.4, f32[2,256,128]{2,1,0:T(8,128)S(1)} %copy-done.6, ...), custom_call_target="tpu_custom_call" | custom-call | tf_op jit(solution)/shard_map/dedisperse/pallas_call | solution.py:356
  34.3 10.3 %all_to_all.16.got_ref = bf16[16,16,128]{2,1,0:T(8,128)(2,1)S(1)} all-to-all(bf16[16,16,128]{2,1,0:T(8,128)(2,1)S(1)} %dedisperse.1), channel_id=1, replica_groups=mesh['beam'=2,'wide'=16] {'wide'}, dimensions={0} | all-to-all | bytes 131072 | tf_op jit(solution)/shard_map/all_to_all | solution.py:370
  44.6 0.0 copy-done.7
  44.6 0.0 copy-done.8
  44.6 0.0 copy-done.9
  44.6 0.9 %inverse.1 = f32[1,1,4096]{2,1,0:T(1,128)} custom-call(bf16[16,16,128]{2,1,0:T(8,128)(2,1)S(1)} %all_to_all.16.got_ref, bf16[128,1024]{1,0:T(8,128)(2,1)S(1)} %copy-done.7, f32[2,8,512]{2,1,0:T(8,128)S(1)} %copy-done.8, f32[8,16]{1,0:T(8,128)S(1)} %copy-done.9), custom_call_target="tpu_custom_call" | custom-call | tf_op jit(solution)/shard_map/inverse/pallas_call | solution.py:373
Async XLA Ops:
  0.0 1.6 %copy-start = (bf16[1,256,4096]{2,1,0:T(8,128)(2,1)S(1)}, bf16[1,256,4096]{2,1,0:T(8,128)(2,1)}, u32[]{:S(2)}) copy-start(bf16[1,256,4096]{2,1,0:T(8,128)(2,1)} %param.9) | copy-start | bytes 6291460
  1.6 0.7 %copy-start.10 = (s32[7]{0:T(128)S(1)}, s32[7]{0:T(128)}, u32[]{:S(2)}) copy-start(s32[7]{0:T(128)} %edges_ref.3) | copy-start | bytes 88
  2.2 0.7 %copy-start.12 = (s32[256]{0:T(256)S(1)}, s32[256]{0:T(256)}, u32[]{:S(2)}) copy-start(s32[256]{0:T(256)} %param.10) | copy-start | bytes 3076
  2.9 15.5 %copy-start.1 = (bf16[1,256,4096]{2,1,0:T(8,128)(2,1)S(1)}, bf16[1,256,4096]{2,1,0:T(8,128)(2,1)}, u32[]{:S(2)}) copy-start(bf16[1,256,4096]{2,1,0:T(8,128)(2,1)} %param.9) | copy-start | bytes 6291460
  4.7 13.7 %all-to-all-start = ((f32[16,1,128]{2,1,0:T(1,128)}), f32[16,1,128]{2,1,0:T(1,128)S(1)}, u32[]{:S(2)}, u32[]{:S(2)}) async-start(f32[16,1,128]{2,1,0:T(1,128)} %bitcast.3), calls=%async_computation | async-start | bytes 16384 | tf_op jit(solution)/shard_map/all_to_all | solution.py:346
  12.1 0.7 %copy-start.13 = (s32[16]{0:T(128)S(1)}, s32[16]{0:T(128)}, u32[]{:S(2)}) copy-start(s32[16]{0:T(128)} %delays_ref.1) | copy-start | bytes 196
  14.7 0.7 %copy-start.3 = (f32[2,256,128]{2,1,0:T(8,128)}, f32[2,256,128]{2,1,0:T(8,128)S(1)}, u32[]{:S(2)}) copy-start(f32[2,256,128]{2,1,0:T(8,128)S(1)} %get-tuple-element.12.base_ref) | copy-start | bytes 786436
  15.4 0.7 %copy-start.5 = (f32[2,256,128]{2,1,0:T(8,128)}, f32[2,256,128]{2,1,0:T(8,128)S(1)}, u32[]{:S(2)}) copy-start(f32[2,256,128]{2,1,0:T(8,128)S(1)} %get-tuple-element.13.turn_ref) | copy-start | bytes 786436
  18.4 1.0 %copy-start.2 = (bf16[2,256,512]{2,1,0:T(8,128)(2,1)S(1)}, bf16[2,256,512]{2,1,0:T(8,128)(2,1)}, u32[]{:S(2)}) copy-start(bf16[2,256,512]{2,1,0:T(8,128)(2,1)} %constant.10.clone.real_ref) | copy-start | bytes 1572868
  19.5 0.9 %copy-start.4 = (f32[2,256,128]{2,1,0:T(8,128)S(1)}, f32[2,256,128]{2,1,0:T(8,128)}, u32[]{:S(2)}) copy-start(f32[2,256,128]{2,1,0:T(8,128)} %copy-done.3) | copy-start | bytes 786436
  20.4 0.9 %copy-start.6 = (f32[2,256,128]{2,1,0:T(8,128)S(1)}, f32[2,256,128]{2,1,0:T(8,128)}, u32[]{:S(2)}) copy-start(f32[2,256,128]{2,1,0:T(8,128)} %copy-done.5) | copy-start | bytes 786436
  21.4 0.7 %copy-start.11 = (s32[7]{0:T(128)S(1)}, s32[7]{0:T(128)}, u32[]{:S(2)}) copy-start(s32[7]{0:T(128)} %edges_ref.3) | copy-start | bytes 88
  22.0 22.6 %copy-start.7 = (bf16[128,1024]{1,0:T(8,128)(2,1)S(1)}, bf16[128,1024]{1,0:T(8,128)(2,1)}, u32[]{:S(2)}) copy-start(bf16[128,1024]{1,0:T(8,128)(2,1)} %constant.12.clone.first_ref) | copy-start | bytes 786436
  22.0 22.6 %copy-start.8 = (f32[2,8,512]{2,1,0:T(8,128)S(1)}, f32[2,8,512]{2,1,0:T(8,128)}, u32[]{:S(2)}) copy-start(f32[2,8,512]{2,1,0:T(8,128)} %constant.13.clone.twiddle_ref) | copy-start | bytes 98308
  22.0 22.6 %copy-start.9 = (f32[8,16]{1,0:T(8,128)S(1)}, f32[8,16]{1,0:T(8,128)}, u32[]{:S(2)}) copy-start(f32[8,16]{1,0:T(8,128)} %constant.14.clone.last_ref) | copy-start | bytes 1540
